TPU v7x, 512 devices: a whole 4x8x8 slice. The times are simulated.
512 devices in a mesh: frame: 32 (over y_hi, x, core), space: 16 (over z, y_lo).
Axes of the slice: x: 4, y: 8 (y_hi: 4, y_lo: 2; y = y_hi * 2 + y_lo), z: 8, core: 2. Of those that a mesh axis runs over, the one named last changes fastest.
Arguments:
- current_image: float32 [64, 16, 160, 2, 160], P('frame', 'space'), may hold values from -6 to 6
- coil_maps: bfloat16 [16, 8, 160, 2, 160], P('space'), may hold values from -2 to 2
- measured_lines: float32 [64, 16, 8, 40, 2, 160], P('frame', 'space'), may hold values from -6 to 6
- sampled_lines: int32 [64, 40], P('frame'), may hold values from 0 to 159, as said below
- prior_weights: float32 [64], replicated, may hold values from 0.2 to 2
- langevin_noise: float32 [64, 16, 160, 2, 160], P('frame', 'space'), may hold values from -2 to 2
Outputs:
- next_image: float32 [64, 16, 160, 2, 160], P('frame', 'space')
Inputs may be any that keep to these rules, and one draw needn't show every extreme that they name: `sampled_lines`: each frame's 40 indices are distinct and include 0 and 159, the lowest phase-encode frequencies.
All inputs are finite; a program needn't handle non-finite values.
Results may differ from a plain program's by a relative error of at most 0.005.
Values sent between devices are 32-bit elements; how exact they have to be, the bound alone decides.
A program may use at most 64 MiB of HBM per device.

v0:
```python
import math
import jax
import jax.numpy as jnp
from jax import lax
from jax.sharding import PartitionSpec as P

step_size = 0.5
coupling = 0.25
softness = 0.01


def with_halo(array, sides, width):
    for axis, dim in sides:
        count, length = (lax.axis_size(axis), array.shape[dim])
        up = [(i, (i + 1) % count) for i in range(count - 1)]
        down = [(j, i) for i, j in up]
        last = lax.slice_in_dim(array, length - width, length, axis=dim)
        initial = lax.slice_in_dim(array, 0, width, axis=dim)
        before = lax.ppermute(last, axis, up)
        after = lax.ppermute(initial, axis, down)
        array = jnp.concatenate([before, array, after], axis=dim)
    return array


def cosine_pair(waves, positions, count):
    product = waves[..., None] * positions % count
    angles = 2.0 * math.pi / count * product.astype(jnp.float32)
    scale = 1.0 / math.sqrt(count)
    return (jnp.cos(angles) * scale, jnp.sin(angles) * scale)


def row_table(count):
    indices = jnp.arange(count, dtype=jnp.int32)
    cosine, sine = cosine_pair(indices, indices, count)
    upper = jnp.concatenate([cosine, -sine], axis=1)
    lower = jnp.concatenate([sine, cosine], axis=1)
    return jnp.concatenate([upper, lower], axis=0).astype(jnp.bfloat16)


def line_table(waves, count):
    positions = jnp.arange(count, dtype=jnp.int32)
    cosine, sine = cosine_pair(waves, positions, count)
    real_part = jnp.stack([cosine, sine], axis=-1)
    imag_part = jnp.stack([-sine, cosine], axis=-1)
    return jnp.stack([real_part, imag_part], axis=-4)


def sense(maps, field):
    map_re = maps[:, :, :, 0, :].astype(jnp.float32)[None]
    map_im = maps[:, :, :, 1, :].astype(jnp.float32)[None]
    field_re = field[:, :, None, :, 0, :]
    field_im = field[:, :, None, :, 1, :]
    coil_real = map_re * field_re - map_im * field_im
    coil_imag = map_re * field_im + map_im * field_re
    return jnp.stack([coil_real, coil_imag], axis=4).astype(jnp.bfloat16)


def combine(maps, back_image):
    map_re = maps[:, :, :, 0, :].astype(jnp.float32)[None]
    map_im = maps[:, :, :, 1, :].astype(jnp.float32)[None]
    back_re = back_image[:, :, :, :, 0, :]
    back_im = back_image[:, :, :, :, 1, :]
    grad_re = jnp.sum(map_re * back_re + map_im * back_im, axis=2)
    grad_im = jnp.sum(map_re * back_im - map_im * back_re, axis=2)
    return jnp.stack([grad_re, grad_im], axis=3)


def on_device(
    current_image, coil_maps, measured_lines, sampled_lines, prior_weights, langevin_noise
):
    frames_dev, slices_dev, height, _, width = current_image.shape
    rotation = row_table(width)
    frame_tables = line_table(sampled_lines, height).astype(jnp.bfloat16)
    coil_image = sense(coil_maps, current_image)
    shape = coil_image.shape
    flat = coil_image.reshape(shape[:4] + (2 * width,))
    row_spectra = (
        jnp.dot(flat, rotation, preferred_element_type=jnp.float32)
        .astype(jnp.bfloat16)
        .reshape(shape)
    )
    estimate = jnp.einsum(
        "folxi,fscxiy->fscloy", frame_tables, row_spectra, preferred_element_type=jnp.float32
    )
    residual = (estimate - measured_lines).astype(jnp.bfloat16)
    back_rows = jnp.einsum(
        "folxi,fscloy->fscxiy", frame_tables, residual, preferred_element_type=jnp.float32
    )
    back_rows = back_rows.astype(jnp.bfloat16)
    back_image = jnp.dot(
        back_rows.reshape(shape[:4] + (2 * width,)), rotation.T, preferred_element_type=jnp.float32
    ).reshape(shape)
    data_grad = combine(coil_maps, back_image)
    total_frames = frames_dev * lax.axis_size("frame")
    time_table = line_table(jnp.arange(total_frames, dtype=jnp.int32), total_frames)
    spectrum = jnp.einsum(
        "okfi,fsxiy->ksxoy",
        time_table,
        lax.all_to_all(current_image, "frame", split_axis=2, concat_axis=0, tiled=True),
        precision=lax.Precision.HIGHEST,
    )
    magnitude = jnp.sqrt(spectrum[:, :, :, 0, :] ** 2 + spectrum[:, :, :, 1, :] ** 2 + softness)
    shrunk = prior_weights[:, None, None, None, None] * spectrum / magnitude[:, :, :, None, :]
    moved = jnp.einsum("okfi,ksxoy->fsxiy", time_table, shrunk, precision=lax.Precision.HIGHEST)
    prior_grad = lax.all_to_all(moved, "frame", split_axis=0, concat_axis=2, tiled=True)
    padded = with_halo(current_image, (("space", 1),), 1)
    slice_grad = coupling * (2.0 * current_image - padded[:, :-2] - padded[:, 2:])
    return current_image - step_size * (data_grad + prior_grad + slice_grad) + langevin_noise


def solution(mesh):
    return jax.shard_map(
        on_device,
        mesh=mesh,
        in_specs=(
            P("frame", "space", None, None, None),
            P("space", None, None, None, None),
            P("frame", "space", None, None, None, None),
            P("frame", None),
            P(),
            P("frame", "space", None, None, None),
        ),
        out_specs=P("frame", "space", None, None, None),
        check_vma=False,
    )
```

profile of v0, /device:TPU:201, one launch (start us, length us, event | category | flops | bytes accessed | tf_op | source)
XLA Modules:
  0.0 109.2 jit_solution(4588862148439000523)
XLA Ops:
  0.0 0.0 copy-start.1
  0.0 2.1 %copy.78 = f32[2,1,160,2,160]{4,2,0,3,1:T(8,128)} copy(f32[2,1,160,2,160]{4,3,2,1,0:T(2,128)} %param.6) | data formatting | bytes 819200 | tf_op args[0]
  2.1 5.1 %collective-permute-start = (f32[2,1,160,2,160]{4,2,0,3,1:T(8,128)}, f32[2,1,160,2,160]{4,2,0,3,1:T(8,128)}, u32[]{:S(2)}, u32[]{:S(2)}) collective-permute-start(f32[2,1,160,2,160]{4,2,0,3,1:T(8,128)} %copy.78), channel_id=1, source_target_pairs={{0,1},{1,2},{2,3},{3,4},{4,5},{5,6},{6,7},{7,8},{8,9},{9,10},{10,1... | collective-permute-start | bytes 1228808 | tf_op jit(solution)/shard_map/ppermute | solution.py:19
  7.2 1.9 %collective-permute-start.1 = (f32[2,1,160,2,160]{4,2,0,3,1:T(8,128)}, f32[2,1,160,2,160]{4,2,0,3,1:T(8,128)}, u32[]{:S(2)}, u32[]{:S(2)}) collective-permute-start(f32[2,1,160,2,160]{4,2,0,3,1:T(8,128)} %copy.78), channel_id=1, source_target_pairs={{1,0},{2,1},{3,2},{4,3},{5,4},{6,5},{7,6},{8,7},{9,8},{10,9},{11,1... | collective-permute-start | bytes 1228808 | tf_op jit(solution)/shard_map/ppermute | solution.py:20
  9.1 2.2 %copy.68 = f32[2,1,160,2,160]{4,3,1,0,2:T(2,128)} copy(f32[2,1,160,2,160]{4,3,2,1,0:T(2,128)} %param.6) | data formatting | bytes 819200 | tf_op args[0]
  11.3 10.7 %all-to-all-start = ((f32[2,1,160,2,160]{4,3,1,0,2:T(2,128)}), f32[2,1,160,2,160]{4,3,1,0,2:T(2,128)S(1)}, u32[]{:S(2)}, u32[]{:S(2)}) async-start(f32[2,1,160,2,160]{4,3,1,0,2:T(2,128)} %copy.68), calls=%async_computation | async-start | bytes 1310720 | tf_op jit(solution)/shard_map/all_to_all | solution.py:99
  22.0 1.1 %slice_bitcast_fusion.3 = (f32[2,160,160]{2,1,0:T(8,128)S(1)}, f32[2,160,160]{2,1,0:T(8,128)S(1)}) fusion(f32[2,1,160,2,160]{4,2,0,3,1:T(8,128)} %copy.78), kind=kLoop, calls=%fused_computation.37 | loop fusion | bytes 819200 | tf_op jit(solution)/shard_map/mul | solution.py:53
  23.1 0.7 negate_convert_fusion
  23.8 0.7 fusion.36
  24.4 0.8 sine_multiply_fusion.2
  25.2 0.8 fusion.53
  25.9 0.0 copy-done.1
  25.9 2.4 %fusion.57 = (bf16[1,8,160,1,160]{4,3,2,1,0:T(2,128)(2,1)S(1)}, bf16[1,8,160,1,160]{4,3,2,1,0:T(2,128)(2,1)S(1)}) fusion(bf16[1,8,160,2,160]{4,3,2,1,0:T(2,128)(2,1)S(1)} %copy-done.1), kind=kLoop, calls=%fused_computation.88 | loop fusion | bytes 1638400 | tf_op jit(solution)/shard_map/slice | solution.py:59
  28.3 0.2 fusion.20
  28.5 5.5 %subtract_convert_fusion = (bf16[2,1,8,160,1,160]{5,4,3,2,0,1:T(2,128)(2,1)S(1)}, bf16[2,1,8,160,1,160]{5,4,3,2,0,1:T(2,128)(2,1)S(1)}) fusion(f32[2,160,160]{2,1,0:T(8,128)S(1)} %get-tuple-element.12, f32[8,160,160]{2,1,0:T(8,128)S(1)} %get-tuple-element.20, f32[2,160,160]{2,1,0:T(8,128)S(1)} %get-tuple-element.11, f32[8,160,160]{2,1,0:T(8,128)S(1)} %get-tuple-element.21), kind=kLoop, calls=%fused_computation.9 | loop fusion | flops 3276800 | bytes 3686400 | tf_op jit(solution)/shard_map/convert.16
  34.0 7.3 %pad_maximum_fusion = bf16[2,1,8,160,2,160]{5,4,3,2,0,1:T(2,128)(2,1)} fusion(bf16[2,1,8,160,1,160]{5,4,3,2,0,1:T(2,128)(2,1)S(1)} %get-tuple-element.8, bf16[2,1,8,160,1,160]{5,4,3,2,0,1:T(2,128)(2,1)S(1)} %get-tuple-element.7), kind=kLoop, calls=%fused_computation.3 | loop fusion | flops 3276800 | bytes 3276800 | tf_op jit(solution)/shard_map/stack | solution.py:55
  41.4 6.6 %convert_element_type.117 = bf16[2,8,160,320]{3,2,1,0:T(8,128)(2,1)} reshape(bf16[2,1,8,160,2,160]{5,4,3,2,0,1:T(2,128)(2,1)} %pad_maximum_fusion) | data formatting | bytes 3276800 | tf_op jit(solution)/shard_map/convert_element_type | solution.py:55
  48.0 0.0 copy-start.2
  48.0 0.0 copy-start.3
  48.0 4.3 %convolution_convert_fusion = bf16[2,8,160,320]{3,2,1,0:T(8,128)(2,1)} fusion(bf16[2,8,160,320]{3,2,1,0:T(8,128)(2,1)} %convert_element_type.117, bf16[160,160]{1,0:T(8,128)(2,1)S(1)} %get-tuple-element.23, bf16[160,160]{1,0:T(8,128)(2,1)S(1)} %fusion.36, bf16[160,160]{1,0:T(8,128)(2,1)S(1)} %get-tuple-element.22), kind=kOutput, calls=%fused_computation.11 | convolution fusion | flops 525926400 | bytes 3430400 | tf_op jit(solution)/shard_map/dot_general | solution.py:78
  52.3 0.0 copy-done.2
  52.3 0.0 copy-done.3
  52.3 0.7 maximum_bitcast_fusion.2
  52.9 7.0 %reshape.357 = bf16[2,8,160,2,160]{4,3,2,1,0:T(2,128)(2,1)} reshape(bf16[2,8,160,320]{3,2,1,0:T(8,128)(2,1)} %convolution_convert_fusion) | data formatting | bytes 3276800 | tf_op jit(solution)/shard_map/reshape.14
  60.0 1.1 %fusion.46 = (bf16[2,40,160,1]{2,1,3,0:T(8,128)(2,1)S(1)}, bf16[2,40,160,1]{2,1,3,0:T(8,128)(2,1)S(1)}, bf16[2,40,160,1]{2,1,3,0:T(8,128)(2,1)S(1)}) fusion(s32[2,40]{1,0:T(2,128)} %param.9), kind=kLoop, calls=%fused_computation.71 | loop fusion | flops 192000 | bytes 77120 | tf_op jit(solution)/shard_map/convert.9
  61.1 0.7 maximum_bitcast_fusion
  61.8 5.1 %bitcast_convert_fusion = bf16[2,8,160,160,2]{3,2,4,1,0:T(8,128)(2,1)} fusion(f32[2,1,8,40,2,160]{5,4,3,2,1,0:T(2,128)} %param.8, bf16[2,8,160,2,160,1]{4,3,2,1,0,5:T(2,128)(2,1)} %bitcast.148, bf16[2,1,40,160,2]{3,2,4,1,0:T(8,128)(2,1)} %get-tuple-element.14, bf16[2,1,40,160,2]{3,2,4,1,0:T(8,128)(2,1)} %get-tuple-element.13), kind=kOutput, calls=%fused_computation | convolution fusion | flops 263628800 | bytes 4198400 | tf_op jit(solution)/shard_map/folxi,fscloy->fscxiy/dot_general | solution.py:86
  66.8 0.0 copy-start.4
  66.8 0.0 all-to-all-done
  66.9 1.2 %copy.141 = f32[2,1,32,5,2,160]{5,0,2,4,3,1:T(2,128)} copy(f32[2,1,32,5,2,160]{5,4,0,3,2,1:T(2,128)S(1)} %bitcast.149) | data formatting | bytes 819200 | tf_op jit(solution)/shard_map/all_to_all | solution.py:99
  68.0 1.5 %reshape.374 = f32[64,5,2,160,1]{3,0,2,1,4:T(8,128)S(1)} reshape(f32[32,2,1,5,2,160]{5,1,0,4,3,2:T(2,128)} %bitcast.150) | data formatting | bytes 819200 | tf_op jit(solution)/shard_map/reshape.23
  69.6 1.6 %convolution_bitcast_fusion.2 = f32[64,1,5,2,160]{4,0,2,3,1:T(8,128)S(1)} fusion(f32[64,5,2,160,1]{3,0,2,1,4:T(8,128)S(1)} %reshape.374, f32[1,64,64,2]{2,1,3,0:T(8,128)} %get-tuple-element.16, f32[1,64,64,2]{2,1,3,0:T(8,128)} %get-tuple-element.15), kind=kOutput, calls=%fused_computation.16 | convolution fusion | flops 157302784 | bytes 884736 | tf_op jit(solution)/shard_map/okfi,fsxiy->ksxoy/dot_general | solution.py:96
  71.2 0.1 fusion.26
  71.3 0.0 copy-done.4
  71.3 1.7 %convolution_bitcast_fusion.1 = f32[64,1,5,2,160]{4,0,3,2,1:T(8,128)S(1)} fusion(f32[64,1,5,2,160]{4,0,2,3,1:T(8,128)S(1)} %convolution_bitcast_fusion.2, f32[64,5,160]{2,0,1:T(8,128)S(1)} %fusion.26, f32[64]{0:T(128)S(1)} %copy-done.4, f32[1,64,64,2]{2,1,3,0:T(8,128)} %get-tuple-element.16, f32[1,64,64,2]{2,1,3,0:T(8,128)} %get-tuple-element.15), kind=kOutput, calls=%fused_computation.15 | convolution fusion | flops 157507584 | bytes 1089792 | tf_op jit(solution)/shard_map/okfi,ksxoy->fsxiy/dot_general | solution.py:104
  73.0 1.4 %copy.72 = f32[64,1,5,2,160]{4,3,2,1,0:T(2,128)} copy(f32[64,1,5,2,160]{4,0,3,2,1:T(8,128)S(1)} %convolution_bitcast_fusion.1) | data formatting | bytes 819200 | tf_op jit(solution)/shard_map/okfi,ksxoy->fsxiy/transpose | solution.py:104
  74.4 9.8 %all-to-all-start.1 = ((f32[64,1,5,2,160]{4,3,2,1,0:T(2,128)}), f32[64,1,5,2,160]{4,3,2,1,0:T(2,128)}, u32[]{:S(2)}, u32[]{:S(2)}) async-start(f32[64,1,5,2,160]{4,3,2,1,0:T(2,128)} %copy.72), calls=%async_computation.1 | async-start | bytes 1310720 | tf_op jit(solution)/shard_map/all_to_all | solution.py:105
  84.2 0.1 maximum_maximum_fusion
  84.4 4.0 %convolution_bitcast_fusion = f32[2,1,8,160,2,160]{5,3,4,2,0,1:T(8,128)S(1)} fusion(bf16[2,8,160,320,1]{2,3,4,1,0:T(8,128)(2,1)} %bitcast.147, bf16[2,160,320,1,1]{2,1,0,4,3:T(8,128)(2,1)S(1)} %bitcast.153), kind=kOutput, calls=%fused_computation.10 | convolution fusion | flops 524288000 | bytes 5120000 | tf_op jit(solution)/shard_map/dot_general | solution.py:90
  88.3 0.0 copy-start
  88.4 1.8 %add_reduce_fusion = (f32[2,160,160]{2,1,0:T(8,128)}, f32[2,160,160]{2,1,0:T(8,128)}) fusion(f32[2,1,8,160,2,160]{5,3,4,2,0,1:T(8,128)S(1)} %convolution_bitcast_fusion, f32[8,160,160]{2,1,0:T(8,128)S(1)} %get-tuple-element.20, f32[8,160,160]{2,1,0:T(8,128)S(1)} %get-tuple-element.21), kind=kLoop, calls=%fused_computation.7 | loop fusion | flops 3174400 | bytes 5324800 | tf_op jit(solution)/shard_map/reduce_sum | solution.py:63
  90.2 14.4 %all-to-all-done.1 = f32[64,1,5,2,160]{4,3,2,1,0:T(2,128)} async-done(((f32[64,1,5,2,160]{4,3,2,1,0:T(2,128)}), f32[64,1,5,2,160]{4,3,2,1,0:T(2,128)}, u32[]{:S(2)}, u32[]{:S(2)}) %all-to-all-start.1) | async-done | bytes 409632 | tf_op jit(solution)/shard_map/all_to_all | solution.py:105
  104.6 1.3 %copy.73 = f32[32,2,1,5,2,160]{5,4,3,0,1,2:T(2,128)S(1)} copy(f32[32,2,1,5,2,160]{5,4,3,1,0,2:T(2,128)} %bitcast.58) | data formatting | bytes 819200 | tf_op jit(solution)/shard_map/all_to_all | solution.py:105
  105.9 0.0 collective-permute-done
  105.9 0.0 collective-permute-done.1
  105.9 0.0 copy-done
  105.9 1.9 %fusion.19 = f32[2,1,160,2,160]{4,2,0,3,1:T(8,128)S(1)} fusion(f32[2,1,160,1,160]{4,2,0,3,1:T(8,128)} %bitcast.152, f32[2,1,160,1,160]{4,2,0,3,1:T(8,128)} %bitcast.151, f32[2,1,160,2,160]{4,3,2,1,0:T(2,128)} %param.11, f32[2,1,160,2,160]{4,3,2,0,1:T(2,128)S(1)} %bitcast.146, f32[2,1,160,2,160]{4,2,0,3,1:T(8,128)} %collective-permute-done.1, ...), kind=kLoop, calls=%fused_computation.22 | loop fusion | flops 1024000 | bytes 2867200 | tf_op jit(solution)/shard_map/add | solution.py:108
  107.9 1.3 %copy.80 = f32[2,1,160,2,160]{4,3,2,1,0:T(2,128)} copy(f32[2,1,160,2,160]{4,2,0,3,1:T(8,128)S(1)} %fusion.19) | data formatting | bytes 819200 | tf_op jit(solution)/shard_map/add | solution.py:108
Async XLA Ops:
  0.0 25.9 %copy-start.1 = (bf16[1,8,160,2,160]{4,3,2,1,0:T(2,128)(2,1)S(1)}, bf16[1,8,160,2,160]{4,3,2,1,0:T(2,128)(2,1)}, u32[]{:S(2)}) copy-start(bf16[1,8,160,2,160]{4,3,2,1,0:T(2,128)(2,1)} %param.7) | copy-start | bytes 2457604
  2.1 103.8 %collective-permute-start = (f32[2,1,160,2,160]{4,2,0,3,1:T(8,128)}, f32[2,1,160,2,160]{4,2,0,3,1:T(8,128)}, u32[]{:S(2)}, u32[]{:S(2)}) collective-permute-start(f32[2,1,160,2,160]{4,2,0,3,1:T(8,128)} %copy.78), channel_id=1, source_target_pairs={{0,1},{1,2},{2,3},{3,4},{4,5},{5,6},{6,7},{7,8},{8,9},{9,10},{10,1... | collective-permute-start | bytes 1228808 | tf_op jit(solution)/shard_map/ppermute | solution.py:19
  7.2 98.7 %collective-permute-start.1 = (f32[2,1,160,2,160]{4,2,0,3,1:T(8,128)}, f32[2,1,160,2,160]{4,2,0,3,1:T(8,128)}, u32[]{:S(2)}, u32[]{:S(2)}) collective-permute-start(f32[2,1,160,2,160]{4,2,0,3,1:T(8,128)} %copy.78), channel_id=1, source_target_pairs={{1,0},{2,1},{3,2},{4,3},{5,4},{6,5},{7,6},{8,7},{9,8},{10,9},{11,1... | collective-permute-start | bytes 1228808 | tf_op jit(solution)/shard_map/ppermute | solution.py:20
  11.3 55.6 %all-to-all-start = ((f32[2,1,160,2,160]{4,3,1,0,2:T(2,128)}), f32[2,1,160,2,160]{4,3,1,0,2:T(2,128)S(1)}, u32[]{:S(2)}, u32[]{:S(2)}) async-start(f32[2,1,160,2,160]{4,3,1,0,2:T(2,128)} %copy.68), calls=%async_computation | async-start | bytes 1310720 | tf_op jit(solution)/shard_map/all_to_all | solution.py:99
  48.0 4.3 %copy-start.2 = (f32[64,64,1]{1,0,2:T(8,128)S(1)}, f32[64,64,1]{1,0,2:T(8,128)}, u32[]{:S(2)}) copy-start(f32[64,64,1]{1,0,2:T(8,128)} %get-tuple-element.25) | copy-start | bytes 49156
  48.0 4.3 %copy-start.3 = (f32[64,64,1]{1,0,2:T(8,128)S(1)}, f32[64,64,1]{1,0,2:T(8,128)}, u32[]{:S(2)}) copy-start(f32[64,64,1]{1,0,2:T(8,128)} %fusion.53) | copy-start | bytes 49156
  66.8 4.5 %copy-start.4 = (f32[64]{0:T(128)S(1)}, f32[64]{0:T(128)}, u32[]{:S(2)}) copy-start(f32[64]{0:T(128)} %param.10) | copy-start | bytes 772
  74.4 30.2 %all-to-all-start.1 = ((f32[64,1,5,2,160]{4,3,2,1,0:T(2,128)}), f32[64,1,5,2,160]{4,3,2,1,0:T(2,128)}, u32[]{:S(2)}, u32[]{:S(2)}) async-start(f32[64,1,5,2,160]{4,3,2,1,0:T(2,128)} %copy.72), calls=%async_computation.1 | async-start | bytes 1310720 | tf_op jit(solution)/shard_map/all_to_all | solution.py:105
  88.3 17.6 %copy-start = (f32[2,1,160,2,160]{4,3,2,1,0:T(2,128)S(1)}, f32[2,1,160,2,160]{4,3,2,1,0:T(2,128)}, u32[]{:S(2)}) copy-start(f32[2,1,160,2,160]{4,3,2,1,0:T(2,128)} %param.6) | copy-start | bytes 1228804
where the time goes:
time: 110 us; the launch traced here: 109 us
  local copies, waits for them, and re-layouts  28.1 us (26%)
  starting transfers between devices  27.5 us (25%)
  other arithmetic  22.4 us (20%)
  matrix products  16.7 us (15%)
  waiting for transfers between devices  14.4 us (13%)
    all_to_all x1, waiting for transfers between devices, on_device(): lax.all_to_all(moved, 'frame', split_axis=0, concat_axis=2, tiled=True)  14.4 us
    all_to_all x1, starting transfers between devices, on_device(): lax.all_to_all(current_image, 'frame', split_axis=2, concat_axis=0, tiled...  10.7 us
    all_to_all x1, starting transfers between devices, on_device(): lax.all_to_all(moved, 'frame', split_axis=0, concat_axis=2, tiled=True)  9.82 us
    another operation x2, local copies, waits for them, and re-layouts  8.55 us
    another operation x4, other arithmetic  7.95 us
    another operation x1, other arithmetic, sense(): return jnp.stack([coil_real, coil_imag], axis=4).astype(jnp.bfloat16)  7.31 us
    convert_element_type x1, local copies, waits for them, and re-layouts, sense(): return jnp.stack([coil_real, coil_imag], axis=4).astype(jnp.bfloat16)  6.64 us
    dot_general x1, matrix products, on_device(): jnp.einsum('folxi,fscloy->fscxiy', frame_tables, residual, preferred_elem...  5.09 us
  transfers between devices with their start and end apart: 4, of which 1 were waited for; matrix products, arithmetic and copies ran while one was open for 57% of the time, Pallas kernels for 0%

commit v1 on v0

--- a/solution.py
+++ b/solution.py
@@ -102,7 +102,10 @@
     magnitude = jnp.sqrt(spectrum[:, :, :, 0, :] ** 2 + spectrum[:, :, :, 1, :] ** 2 + softness)
     shrunk = prior_weights[:, None, None, None, None] * spectrum / magnitude[:, :, :, None, :]
     moved = jnp.einsum("okfi,ksxoy->fsxiy", time_table, shrunk, precision=lax.Precision.HIGHEST)
-    prior_grad = lax.all_to_all(moved, "frame", split_axis=0, concat_axis=2, tiled=True)
+    prior_grad = jnp.concatenate(
+        lax.all_to_all(jnp.stack(jnp.split(moved, lax.axis_size("frame"), axis=0)), "frame", 0, 0),
+        axis=2,
+    )
     padded = with_halo(current_image, (("space", 1),), 1)
     slice_grad = coupling * (2.0 * current_image - padded[:, :-2] - padded[:, 2:])
     return current_image - step_size * (data_grad + prior_grad + slice_grad) + langevin_noise

time: 110 us -> 128 us (1.16)
  the two profiles are of different devices: /device:TPU:201 before, /device:TPU:1 now
where the time goes in v1:
time: 128 us; the launch traced here: 127 us
  local copies, waits for them, and re-layouts  45 us (35%)
  starting transfers between devices  27.7 us (22%)
  other arithmetic  22.7 us (18%)
  matrix products  16.7 us (13%)
  waiting for transfers between devices  14.6 us (11%)
    unnamed x43, local copies, waits for them, and re-layouts  23.2 us
    all_to_all x1, waiting for transfers between devices, on_device(): lax.all_to_all(jnp.stack(jnp.split(moved, lax.axis_size('frame'), axis=0)...  14.6 us
    all_to_all x1, starting transfers between devices, on_device(): lax.all_to_all(current_image, 'frame', split_axis=2, concat_axis=0, tiled...  11.1 us
    all_to_all x1, starting transfers between devices, on_device(): lax.all_to_all(jnp.stack(jnp.split(moved, lax.axis_size('frame'), axis=0)...  9.84 us
    another operation x2, local copies, waits for them, and re-layouts  8.55 us
    another operation x4, other arithmetic  8.04 us
    another operation x1, other arithmetic, sense(): return jnp.stack([coil_real, coil_imag], axis=4).astype(jnp.bfloat16)  7.31 us
    convert_element_type x1, local copies, waits for them, and re-layouts, sense(): return jnp.stack([coil_real, coil_imag], axis=4).astype(jnp.bfloat16)  6.64 us
  transfers between devices with their start and end apart: 4, of which 1 were waited for; matrix products, arithmetic and copies ran while one was open for 62% of the time, Pallas kernels for 0%

profile of v1, /device:TPU:1, one launch (start us, length us, event | category | flops | bytes accessed | tf_op | source)
XLA Modules:
  0.0 126.9 jit_solution(1992241632169878377)
XLA Ops:
  0.0 2.1 %copy.55 = f32[2,1,160,2,160]{4,2,0,3,1:T(8,128)} copy(f32[2,1,160,2,160]{4,3,2,1,0:T(2,128)} %param.6) | data formatting | bytes 819200 | tf_op args[0]
  2.1 1.3 %collective-permute-start.1 = (f32[2,1,160,2,160]{4,2,0,3,1:T(8,128)}, f32[2,1,160,2,160]{4,2,0,3,1:T(8,128)}, u32[]{:S(2)}, u32[]{:S(2)}) collective-permute-start(f32[2,1,160,2,160]{4,2,0,3,1:T(8,128)} %copy.55), channel_id=1, source_target_pairs={{1,0},{2,1},{3,2},{4,3},{5,4},{6,5},{7,6},{8,7},{9,8},{10,9},{11,1... | collective-permute-start | bytes 1228808 | tf_op jit(solution)/shard_map/ppermute | solution.py:20
  3.4 5.5 %collective-permute-start = (f32[2,1,160,2,160]{4,2,0,3,1:T(8,128)}, f32[2,1,160,2,160]{4,2,0,3,1:T(8,128)}, u32[]{:S(2)}, u32[]{:S(2)}) collective-permute-start(f32[2,1,160,2,160]{4,2,0,3,1:T(8,128)} %copy.55), channel_id=1, source_target_pairs={{0,1},{1,2},{2,3},{3,4},{4,5},{5,6},{6,7},{7,8},{8,9},{9,10},{10,1... | collective-permute-start | bytes 1228808 | tf_op jit(solution)/shard_map/ppermute | solution.py:19
  8.9 2.2 %copy.47 = f32[2,1,160,2,160]{4,3,1,0,2:T(2,128)} copy(f32[2,1,160,2,160]{4,3,2,1,0:T(2,128)} %param.6) | data formatting | bytes 819200 | tf_op args[0]
  11.1 11.1 %all-to-all-start = ((f32[2,1,160,2,160]{4,3,1,0,2:T(2,128)}), f32[2,1,160,2,160]{4,3,1,0,2:T(2,128)S(1)}, u32[]{:S(2)}, u32[]{:S(2)}) async-start(f32[2,1,160,2,160]{4,3,1,0,2:T(2,128)} %copy.47), calls=%async_computation | async-start | bytes 1310720 | tf_op jit(solution)/shard_map/all_to_all | solution.py:99
  22.2 1.1 slice_bitcast_fusion.3
  23.3 0.7 negate_convert_fusion
  24.0 0.7 fusion.36
  24.7 0.8 sine_multiply_fusion.2
  25.4 0.8 fusion.53
  26.2 2.4 %fusion.57 = (bf16[1,8,160,1,160]{4,3,2,1,0:T(2,128)(2,1)S(1)}, bf16[1,8,160,1,160]{4,3,2,1,0:T(2,128)(2,1)S(1)}) fusion(bf16[1,8,160,2,160]{4,3,2,1,0:T(2,128)(2,1)S(1)} %copy-done.1), kind=kLoop, calls=%fused_computation.152 | loop fusion | bytes 1638400 | tf_op jit(solution)/shard_map/slice | solution.py:59
  28.5 0.3 fusion.20
  28.8 5.6 %subtract_convert_fusion = (bf16[2,1,8,160,1,160]{5,4,3,2,0,1:T(2,128)(2,1)S(1)}, bf16[2,1,8,160,1,160]{5,4,3,2,0,1:T(2,128)(2,1)S(1)}) fusion(f32[2,160,160]{2,1,0:T(8,128)S(1)} %get-tuple-element.12, f32[8,160,160]{2,1,0:T(8,128)S(1)} %get-tuple-element.20, f32[2,160,160]{2,1,0:T(8,128)S(1)} %get-tuple-element.11, f32[8,160,160]{2,1,0:T(8,128)S(1)} %get-tuple-element.21), kind=kLoop, calls=%fused_computation.9 | loop fusion | flops 3276800 | bytes 3686400 | tf_op jit(solution)/shard_map/convert.16
  34.4 7.3 %pad_maximum_fusion = bf16[2,1,8,160,2,160]{5,4,3,2,0,1:T(2,128)(2,1)} fusion(bf16[2,1,8,160,1,160]{5,4,3,2,0,1:T(2,128)(2,1)S(1)} %get-tuple-element.8, bf16[2,1,8,160,1,160]{5,4,3,2,0,1:T(2,128)(2,1)S(1)} %get-tuple-element.7), kind=kLoop, calls=%fused_computation.3 | loop fusion | flops 3276800 | bytes 3276800 | tf_op jit(solution)/shard_map/stack | solution.py:55
  41.7 6.6 %convert_element_type.117 = bf16[2,8,160,320]{3,2,1,0:T(8,128)(2,1)} reshape(bf16[2,1,8,160,2,160]{5,4,3,2,0,1:T(2,128)(2,1)} %pad_maximum_fusion) | data formatting | bytes 3276800 | tf_op jit(solution)/shard_map/convert_element_type | solution.py:55
  48.3 4.3 %convolution_convert_fusion = bf16[2,8,160,320]{3,2,1,0:T(8,128)(2,1)} fusion(bf16[2,8,160,320]{3,2,1,0:T(8,128)(2,1)} %convert_element_type.117, bf16[160,160]{1,0:T(8,128)(2,1)S(1)} %get-tuple-element.23, bf16[160,160]{1,0:T(8,128)(2,1)S(1)} %fusion.36, bf16[160,160]{1,0:T(8,128)(2,1)S(1)} %get-tuple-element.22), kind=kOutput, calls=%fused_computation.11 | convolution fusion | flops 525926400 | bytes 3430400 | tf_op jit(solution)/shard_map/dot_general | solution.py:78
  52.6 0.7 maximum_bitcast_fusion.2
  53.3 7.0 %reshape.363 = bf16[2,8,160,2,160]{4,3,2,1,0:T(2,128)(2,1)} reshape(bf16[2,8,160,320]{3,2,1,0:T(8,128)(2,1)} %convolution_convert_fusion) | data formatting | bytes 3276800 | tf_op jit(solution)/shard_map/reshape.16
  60.3 1.1 fusion.46
  61.4 0.7 maximum_bitcast_fusion
  62.1 5.1 %bitcast_convert_fusion = bf16[2,8,160,160,2]{3,2,4,1,0:T(8,128)(2,1)} fusion(f32[2,1,8,40,2,160]{5,4,3,2,1,0:T(2,128)} %param.8, bf16[2,8,160,2,160,1]{4,3,2,1,0,5:T(2,128)(2,1)} %bitcast.274, bf16[2,1,40,160,2]{3,2,4,1,0:T(8,128)(2,1)} %get-tuple-element.14, bf16[2,1,40,160,2]{3,2,4,1,0:T(8,128)(2,1)} %get-tuple-element.13), kind=kOutput, calls=%fused_computation | convolution fusion | flops 263628800 | bytes 4198400 | tf_op jit(solution)/shard_map/folxi,fscloy->fscxiy/dot_general | solution.py:86
  67.2 1.2 copy.118
  68.4 1.5 %reshape.382 = f32[64,5,2,160,1]{3,0,2,1,4:T(8,128)S(1)} reshape(f32[32,2,1,5,2,160]{5,1,0,4,3,2:T(2,128)} %bitcast.276) | data formatting | bytes 819200 | tf_op jit(solution)/shard_map/reshape.25
  69.9 1.6 %convolution_bitcast_fusion.2 = f32[64,1,5,2,160]{4,0,2,3,1:T(8,128)S(1)} fusion(f32[64,5,2,160,1]{3,0,2,1,4:T(8,128)S(1)} %reshape.382, f32[1,64,64,2]{2,1,3,0:T(8,128)} %get-tuple-element.16, f32[1,64,64,2]{2,1,3,0:T(8,128)} %get-tuple-element.15), kind=kOutput, calls=%fused_computation.16 | convolution fusion | flops 157302784 | bytes 884736 | tf_op jit(solution)/shard_map/okfi,fsxiy->ksxoy/dot_general | solution.py:96
  71.5 0.1 fusion.26
  71.7 1.7 %convolution_bitcast_fusion.1 = f32[64,1,5,2,160]{4,0,3,2,1:T(8,128)S(1)} fusion(f32[64,1,5,2,160]{4,0,2,3,1:T(8,128)S(1)} %convolution_bitcast_fusion.2, f32[64,5,160]{2,0,1:T(8,128)S(1)} %fusion.26, f32[64]{0:T(128)S(1)} %copy-done.4, f32[1,64,64,2]{2,1,3,0:T(8,128)} %get-tuple-element.16, f32[1,64,64,2]{2,1,3,0:T(8,128)} %get-tuple-element.15), kind=kOutput, calls=%fused_computation.15 | convolution fusion | flops 157507584 | bytes 1089792 | tf_op jit(solution)/shard_map/okfi,ksxoy->fsxiy/dot_general | solution.py:104
  73.4 0.6 constant_dynamic-update-slice_fusion.31
  74.0 0.6 constant_dynamic-update-slice_fusion.30
  74.6 0.6 constant_dynamic-update-slice_fusion.29
  75.2 0.6 constant_dynamic-update-slice_fusion.28
  75.8 0.6 constant_dynamic-update-slice_fusion.27
  76.4 0.6 constant_dynamic-update-slice_fusion.26
  77.1 0.6 constant_dynamic-update-slice_fusion.25
  77.7 0.6 constant_dynamic-update-slice_fusion.24
  78.3 0.6 constant_dynamic-update-slice_fusion.23
  78.9 0.6 constant_dynamic-update-slice_fusion.22
  79.5 0.6 constant_dynamic-update-slice_fusion.21
  80.1 0.6 constant_dynamic-update-slice_fusion.20
  80.7 0.6 constant_dynamic-update-slice_fusion.19
  81.3 0.6 constant_dynamic-update-slice_fusion.18
  82.0 0.6 constant_dynamic-update-slice_fusion.17
  82.6 0.6 constant_dynamic-update-slice_fusion.16
  83.2 0.6 constant_dynamic-update-slice_fusion.15
  83.8 0.6 constant_dynamic-update-slice_fusion.14
  84.4 0.6 constant_dynamic-update-slice_fusion.13
  85.0 0.6 constant_dynamic-update-slice_fusion.12
  85.6 0.6 constant_dynamic-update-slice_fusion.11
  86.2 0.6 constant_dynamic-update-slice_fusion.10
  86.8 0.6 constant_dynamic-update-slice_fusion.9
  87.4 0.6 constant_dynamic-update-slice_fusion.8
  88.1 0.6 constant_dynamic-update-slice_fusion.7
  88.7 0.6 constant_dynamic-update-slice_fusion.6
  89.3 0.6 constant_dynamic-update-slice_fusion.5
  89.9 0.6 constant_dynamic-update-slice_fusion.4
  90.5 0.6 constant_dynamic-update-slice_fusion.3
  91.1 0.6 constant_dynamic-update-slice_fusion.2
  91.7 0.6 constant_dynamic-update-slice_fusion.1
  92.3 0.6 constant_dynamic-update-slice_fusion
  92.9 9.8 %all-to-all-start.1 = ((f32[32,2,1,5,2,160]{5,1,4,3,2,0:T(2,128)}), f32[32,2,1,5,2,160]{5,1,4,3,2,0:T(2,128)}, u32[]{:S(2)}, u32[]{:S(2)}) async-start(f32[32,2,1,5,2,160]{5,1,4,3,2,0:T(2,128)} %constant_dynamic-update-slice_fusion), calls=%async_computation.1 | async-start | bytes 1310720 | tf_op jit(solution)/shard_map/all_to_all | solution.py:106
  102.9 4.0 %convolution_bitcast_fusion = f32[2,1,8,160,2,160]{5,3,4,2,0,1:T(8,128)S(1)} fusion(bf16[2,8,160,320,1]{2,3,4,1,0:T(8,128)(2,1)} %bitcast.273, bf16[2,160,320,1,1]{2,1,0,4,3:T(8,128)(2,1)S(1)} %bitcast.279), kind=kOutput, calls=%fused_computation.10 | convolution fusion | flops 524288000 | bytes 5120000 | tf_op jit(solution)/shard_map/dot_general | solution.py:90
  106.9 1.8 %add_reduce_fusion = (f32[2,160,160]{2,1,0:T(8,128)}, f32[2,160,160]{2,1,0:T(8,128)}) fusion(f32[2,1,8,160,2,160]{5,3,4,2,0,1:T(8,128)S(1)} %convolution_bitcast_fusion, f32[8,160,160]{2,1,0:T(8,128)S(1)} %get-tuple-element.20, f32[8,160,160]{2,1,0:T(8,128)S(1)} %get-tuple-element.21), kind=kLoop, calls=%fused_computation.7 | loop fusion | flops 3174400 | bytes 5324800 | tf_op jit(solution)/shard_map/reduce_sum | solution.py:63
  108.8 14.6 %all-to-all-done.1 = f32[32,2,1,5,2,160]{5,1,4,3,2,0:T(2,128)} async-done(((f32[32,2,1,5,2,160]{5,1,4,3,2,0:T(2,128)}), f32[32,2,1,5,2,160]{5,1,4,3,2,0:T(2,128)}, u32[]{:S(2)}, u32[]{:S(2)}) %all-to-all-start.1) | async-done | bytes 409632 | tf_op jit(solution)/shard_map/all_to_all | solution.py:106
  123.4 2.2 %fusion.19 = f32[2,1,160,2,160]{4,2,0,3,1:T(8,128)S(1)} fusion(f32[2,1,160,1,160]{4,2,0,3,1:T(8,128)} %bitcast.278, f32[2,1,160,1,160]{4,2,0,3,1:T(8,128)} %bitcast.277, f32[2,1,160,2,160]{4,3,2,1,0:T(2,128)} %param.11, f32[2,1,160,2,160]{4,0,3,2,1:T(2,128)} %bitcast.92, f32[2,1,160,2,160]{4,2,0,3,1:T(8,128)} %collective-permute-done.1, ...), kind=kLoop, calls=%fused_computation.22 | loop fusion | flops 1024000 | bytes 2867200 | tf_op jit(solution)/shard_map/add | solution.py:111
  125.6 1.3 %copy.57 = f32[2,1,160,2,160]{4,3,2,1,0:T(2,128)} copy(f32[2,1,160,2,160]{4,2,0,3,1:T(8,128)S(1)} %fusion.19) | data formatting | bytes 819200 | tf_op jit(solution)/shard_map/add | solution.py:111
  (14 shorter events, 0.1 us)
Async XLA Ops:
  0.0 26.2 %copy-start.1 = (bf16[1,8,160,2,160]{4,3,2,1,0:T(2,128)(2,1)S(1)}, bf16[1,8,160,2,160]{4,3,2,1,0:T(2,128)(2,1)}, u32[]{:S(2)}) copy-start(bf16[1,8,160,2,160]{4,3,2,1,0:T(2,128)(2,1)} %param.7) | copy-start | bytes 2457604
  2.1 106.7 %collective-permute-start.1 = (f32[2,1,160,2,160]{4,2,0,3,1:T(8,128)}, f32[2,1,160,2,160]{4,2,0,3,1:T(8,128)}, u32[]{:S(2)}, u32[]{:S(2)}) collective-permute-start(f32[2,1,160,2,160]{4,2,0,3,1:T(8,128)} %copy.55), channel_id=1, source_target_pairs={{1,0},{2,1},{3,2},{4,3},{5,4},{6,5},{7,6},{8,7},{9,8},{10,9},{11,1... | collective-permute-start | bytes 1228808 | tf_op jit(solution)/shard_map/ppermute | solution.py:20
  3.4 105.4 %collective-permute-start = (f32[2,1,160,2,160]{4,2,0,3,1:T(8,128)}, f32[2,1,160,2,160]{4,2,0,3,1:T(8,128)}, u32[]{:S(2)}, u32[]{:S(2)}) collective-permute-start(f32[2,1,160,2,160]{4,2,0,3,1:T(8,128)} %copy.55), channel_id=1, source_target_pairs={{0,1},{1,2},{2,3},{3,4},{4,5},{5,6},{6,7},{7,8},{8,9},{9,10},{10,1... | collective-permute-start | bytes 1228808 | tf_op jit(solution)/shard_map/ppermute | solution.py:19
  11.1 56.1 %all-to-all-start = ((f32[2,1,160,2,160]{4,3,1,0,2:T(2,128)}), f32[2,1,160,2,160]{4,3,1,0,2:T(2,128)S(1)}, u32[]{:S(2)}, u32[]{:S(2)}) async-start(f32[2,1,160,2,160]{4,3,1,0,2:T(2,128)} %copy.47), calls=%async_computation | async-start | bytes 1310720 | tf_op jit(solution)/shard_map/all_to_all | solution.py:99
  48.3 4.3 %copy-start.2 = (f32[64,64,1]{1,0,2:T(8,128)S(1)}, f32[64,64,1]{1,0,2:T(8,128)}, u32[]{:S(2)}) copy-start(f32[64,64,1]{1,0,2:T(8,128)} %get-tuple-element.25) | copy-start | bytes 49156
  48.3 4.3 %copy-start.3 = (f32[64,64,1]{1,0,2:T(8,128)S(1)}, f32[64,64,1]{1,0,2:T(8,128)}, u32[]{:S(2)}) copy-start(f32[64,64,1]{1,0,2:T(8,128)} %fusion.53) | copy-start | bytes 49156
  67.2 4.5 %copy-start.4 = (f32[64]{0:T(128)S(1)}, f32[64]{0:T(128)}, u32[]{:S(2)}) copy-start(f32[64]{0:T(128)} %param.10) | copy-start | bytes 772
  92.9 30.4 %all-to-all-start.1 = ((f32[32,2,1,5,2,160]{5,1,4,3,2,0:T(2,128)}), f32[32,2,1,5,2,160]{5,1,4,3,2,0:T(2,128)}, u32[]{:S(2)}, u32[]{:S(2)}) async-start(f32[32,2,1,5,2,160]{5,1,4,3,2,0:T(2,128)} %constant_dynamic-update-slice_fusion), calls=%async_computation.1 | async-start | bytes 1310720 | tf_op jit(solution)/shard_map/all_to_all | solution.py:106
  106.9 16.5 %copy-start = (f32[2,1,160,2,160]{4,3,2,1,0:T(2,128)S(1)}, f32[2,1,160,2,160]{4,3,2,1,0:T(2,128)}, u32[]{:S(2)}) copy-start(f32[2,1,160,2,160]{4,3,2,1,0:T(2,128)} %param.6) | copy-start | bytes 1228804
